TPU v7x, 128 devices: a whole 4x4x4 slice. The times are simulated.
128 devices in a mesh: outer: 32 (over z, y, core), grp: 4 (over x).
Axes of the slice: x: 4, y: 4, z: 4, core: 2. Of those that a mesh axis runs over, the one named last changes fastest.
Arguments:
- link_ids: int32 [98304, 8], P(('outer', 'grp')), may hold values from 0 to 98303, as said below
- path_states: bfloat16 [98304, 8, 128], P(('outer', 'grp')), may hold values from -1 to 1
- final_grad: bfloat16 [98304, 128], P(('outer', 'grp')), may hold values from -6 to 6
- link_states: bfloat16 [98304, 128], P(('outer', 'grp')), may hold values from -6 to 6
- agg_grad: bfloat16 [98304, 128], P(('outer', 'grp')), may hold values from -3 to 3
- w_in: bfloat16 [128, 384], replicated, may hold values from -0.5 to 0.5
- w_rec: bfloat16 [128, 384], replicated, may hold values from -0.5 to 0.5
- b_in: float32 [384], replicated, may hold values from -1 to 1
- b_rec: float32 [384], replicated, may hold values from -1 to 1
Outputs:
- path_grad: bfloat16 [98304, 128], P(('outer', 'grp'))
- link_grad: float32 [98304, 128], P(('outer', 'grp'))
- w_in_grad: float32 [128, 384], replicated
- w_rec_grad: float32 [128, 384], replicated
- b_in_grad: float32 [384], replicated
- b_rec_grad: float32 [384], replicated
Inputs may be any that keep to these rules, and one draw needn't show every extreme that they name: `link_ids`: within the 6144 hops of each device's paths (aligned blocks), at most 72 lie on links of any one owner (owner = id // 768), and exactly 72 for some owner in every block.
All inputs are finite; a program needn't handle non-finite values.
Results may differ from a plain program's by a relative error of at most 0.0035.
Values may be sent and summed in bfloat16 or wider, within the bound.
A program may use at most 128 MiB of HBM per device.

v0:
```python
import math
import jax
import jax.numpy as jnp
from jax import lax
from jax.sharding import PartitionSpec as P


def gru_backward(carry_grad, inputs, states, w_in, w_rec, b_in, b_rec):
    width = states.shape[-1]
    from_input = jnp.dot(inputs, w_in, preferred_element_type=jnp.float32) + b_in
    from_state = jnp.dot(states, w_rec, preferred_element_type=jnp.float32) + b_rec
    update_gate = jax.nn.sigmoid(from_input[:, :width] + from_state[:, :width])
    reset_gate = jax.nn.sigmoid(from_input[:, width : 2 * width] + from_state[:, width : 2 * width])
    recur_part = from_state[:, 2 * width :]
    candidate = jnp.tanh(from_input[:, 2 * width :] + reset_gate * recur_part)
    state_wide = states.astype(jnp.float32)
    cand_pre = carry_grad * (1.0 - update_gate) * (1.0 - candidate * candidate)
    update_pre = carry_grad * (state_wide - candidate) * update_gate * (1.0 - update_gate)
    reset_pre = cand_pre * recur_part * reset_gate * (1.0 - reset_gate)
    input_pre = jnp.concatenate([update_pre, reset_pre, cand_pre], axis=1).astype(jnp.bfloat16)
    state_pre = jnp.concatenate([update_pre, reset_pre, cand_pre * reset_gate], axis=1).astype(
        jnp.bfloat16
    )
    input_grad = jnp.dot(input_pre, w_in.T, preferred_element_type=jnp.float32)
    state_grad = carry_grad * update_gate + jnp.dot(
        state_pre, w_rec.T, preferred_element_type=jnp.float32
    )
    w_in_term = jnp.dot(inputs.T, input_pre, preferred_element_type=jnp.float32)
    w_rec_term = jnp.dot(states.T, state_pre, preferred_element_type=jnp.float32)
    b_in_term = jnp.sum(input_pre.astype(jnp.float32), axis=0)
    b_rec_term = jnp.sum(state_pre.astype(jnp.float32), axis=0)
    return (state_grad, input_grad, w_in_term, w_rec_term, b_in_term, b_rec_term)


def per_device(link_ids, path_states, final_grad, link_states, agg_grad, w_in, w_rec, b_in, b_rec):
    path_count, hop_count = link_ids.shape
    width = link_states.shape[1]
    row_count = path_count * hop_count
    devices = lax.axis_size(("outer", "grp"))
    capacity = 3 * row_count // (2 * devices)
    links_dev = link_states.shape[0]
    flat_ids = jnp.transpose(link_ids).reshape(row_count)
    owners = flat_ids // links_dev
    local_ids = flat_ids - owners * links_dev
    by_owner = jnp.argsort(owners, stable=True)
    sorted_owners = owners[by_owner]
    group_starts = jnp.searchsorted(
        sorted_owners, jnp.arange(devices, dtype=jnp.int32), side="left"
    )
    slot_sorted = (
        sorted_owners * capacity
        + jnp.arange(row_count, dtype=jnp.int32)
        - group_starts[sorted_owners]
    )
    slots = jnp.zeros((row_count,), jnp.int32).at[by_owner].set(slot_sorted)
    requests = jnp.full((devices * capacity,), links_dev, jnp.int32).at[slots].set(local_ids)
    requests = requests.reshape(devices, capacity)
    link_table = jnp.concatenate([link_states, agg_grad], axis=1)
    asked_ids = lax.all_to_all(requests, ("outer", "grp"), split_axis=0, concat_axis=0, tiled=True)
    clipped = jnp.minimum(asked_ids, links_dev - 1)
    returned = lax.all_to_all(
        link_table[clipped], ("outer", "grp"), split_axis=0, concat_axis=0, tiled=True
    )
    fetched = returned.reshape(devices * capacity, 2 * width)[slots].reshape(
        hop_count, path_count, 2 * width
    )
    carry_grad = final_grad.astype(jnp.float32)
    w_in_sum = jnp.zeros(w_in.shape, jnp.float32)
    w_rec_sum = jnp.zeros(w_rec.shape, jnp.float32)
    b_in_sum = jnp.zeros(b_in.shape, jnp.float32)
    b_rec_sum = jnp.zeros(b_rec.shape, jnp.float32)
    hop_grads = [None] * hop_count
    for hop in range(hop_count - 1, -1, -1):
        hop_rows = fetched[hop]
        carry_grad = carry_grad + hop_rows[:, width:].astype(jnp.float32)
        carry_grad, input_grad, w_in_term, w_rec_term, b_in_term, b_rec_term = gru_backward(
            carry_grad, hop_rows[:, :width], path_states[:, hop], w_in, w_rec, b_in, b_rec
        )
        hop_grads[hop] = input_grad
        w_in_sum = w_in_sum + w_in_term
        w_rec_sum = w_rec_sum + w_rec_term
        b_in_sum = b_in_sum + b_in_term
        b_rec_sum = b_rec_sum + b_rec_term
    grad_rows_all = jnp.stack(hop_grads, axis=0).reshape(row_count, width)
    outgoing = jnp.zeros((devices * capacity, width), jnp.float32).at[slots].set(grad_rows_all)
    incoming = lax.all_to_all(
        outgoing.reshape(devices, capacity, width).astype(jnp.bfloat16),
        ("outer", "grp"),
        split_axis=0,
        concat_axis=0,
        tiled=True,
    ).astype(jnp.float32)
    link_grad = (
        jnp.zeros((links_dev, width), jnp.float32)
        .at[asked_ids.reshape(-1)]
        .add(incoming.reshape(devices * capacity, width), mode="drop")
    )
    w_in_all, w_rec_all, b_in_all, b_rec_all = lax.psum(
        (w_in_sum, w_rec_sum, b_in_sum, b_rec_sum), ("outer", "grp")
    )
    norm_scale = 1.0 / math.sqrt(row_count * devices)
    return (
        carry_grad.astype(jnp.bfloat16),
        link_grad,
        w_in_all * norm_scale,
        w_rec_all * norm_scale,
        b_in_all * norm_scale,
        b_rec_all * norm_scale,
    )


def solution(mesh):
    placed = (
        P(("outer", "grp"), None),
        P(("outer", "grp"), None, None),
        P(("outer", "grp"), None),
        P(("outer", "grp"), None),
        P(("outer", "grp"), None),
        P(),
        P(),
        P(),
        P(),
    )
    return jax.shard_map(
        per_device,
        mesh=mesh,
        in_specs=placed,
        out_specs=(P(("outer", "grp"), None), P(("outer", "grp"), None), P(), P(), P(), P()),
        check_vma=False,
    )
```

profile of v0, /device:TPU:1, one launch (start us, length us, event | category | flops | bytes accessed | tf_op | source)
XLA Modules:
  0.0 602.4 jit_solution(14700198796793534372)
XLA Ops:
  8.0 6.7 %sort.17 = (s32[6144]{0:T(1024)}, s32[6144]{0:T(1024)S(1)}) sort(s32[6144]{0:T(1024)S(1)} %get-tuple-element.208, s32[6144]{0:T(1024)S(1)} %iota.10), dimensions={0}, to_apply=%region_0.1 | sort | flops 79872 | bytes 98304 | tf_op jit(solution)/shard_map/jit(argsort)/sort | solution.py:45
  14.8 34.3 %gather_fusion.1 = s32[6144]{0:T(1024)S(1)} fusion(s32[6144]{0:T(1024)S(1)} %get-tuple-element.208, s32[6144]{0:T(1024)S(1)} %get-tuple-element.209), kind=kCustom, calls=%fused_computation.1 | custom fusion | bytes 73728 | tf_op jit(solution)/shard_map/gather | solution.py:46
  49.1 15.8 %while.24 = (s32[]{:T(128)}, u32[128]{0:T(128)S(1)}, u32[128]{0:T(128)S(1)}, s32[6144]{0:T(1024)S(1)}, s32[]{:T(128)}, /*index=5*/s32[]{:T(128)}, s32[]{}) while((s32[]{:T(128)}, u32[128]{0:T(128)S(1)}, u32[128]{0:T(128)S(1)}, s32[6144]{0:T(1024)S(1)}, s32[]{:T(128)}, /*index=5*/s32[]{:T(128)}, s32[]{}) %tuple.107), condition=%wide.region_2.3_spmd.clone, body=%wide.region_1.2_spmd.clone.sunk | while | flops 2692 | bytes 10340 | solution.py:47
  65.0 36.8 %gather_fusion.2 = s32[6144]{0:T(1024)S(1)} fusion(s32[128]{0:T(128)S(1)} %convert_element_type.136, s32[6144]{0:T(1024)S(1)} %broadcast_clamp_fusion.2), kind=kCustom, calls=%fused_computation.2 | custom fusion | bytes 73728 | tf_op jit(solution)/shard_map/gather | solution.py:53
  101.8 23.0 %scatter_custom_fusion = s32[6144]{0:T(1024)S(1)} fusion(s32[6144]{0:T(1024)S(1)} %get-tuple-element.210, s32[6144]{0:T(1024)S(1)} %add_subtract_fusion, s32[]{:T(128)} %constant.53.clone.1), kind=kCustom, calls=%fused_computation.309 | custom fusion | bytes 24580 | tf_op jit(solution)/shard_map/scatter | solution.py:55
  125.4 23.0 %scatter_custom_fusion.1 = s32[9216]{0:T(1024)S(1)} fusion(s32[6144]{0:T(1024)S(1)} %get-tuple-element.206, s32[6144]{0:T(1024)S(1)} %get-tuple-element.207, s32[]{:T(128)} %constant.52.clone.1), kind=kCustom, calls=%fused_computation.304 | custom fusion | bytes 36868 | tf_op jit(solution)/shard_map/scatter | solution.py:56
  149.1 11.5 %all-to-all-start = ((s32[128,1,72]{2,1,0:T(1,128)}), s32[128,1,72]{2,1,0:T(1,128)S(1)}, u32[]{:S(2)}, u32[]{:S(2)}) async-start(s32[128,1,72]{2,1,0:T(1,128)} %bitcast.3), calls=%async_computation | async-start | bytes 131072 | tf_op jit(solution)/shard_map/all_to_all | solution.py:59
  160.7 9.5 %all-to-all-done = s32[128,1,72]{2,1,0:T(1,128)S(1)} async-done(((s32[128,1,72]{2,1,0:T(1,128)}), s32[128,1,72]{2,1,0:T(1,128)S(1)}, u32[]{:S(2)}, u32[]{:S(2)}) %all-to-all-start) | async-done | bytes 36896 | tf_op jit(solution)/shard_map/all_to_all | solution.py:59
  170.8 1.5 fusion.155
  172.4 36.9 %gather_fusion.3 = bf16[9216,256]{1,0:T(8,128)(2,1)} fusion(bf16[768,256]{1,0:T(8,128)(2,1)S(1)} %pad_maximum_fusion.24, s32[9216]{0:T(1024)S(1)} %broadcast_clamp_fusion), kind=kCustom, calls=%fused_computation.3 | custom fusion | bytes 9474048 | tf_op jit(solution)/shard_map/gather | solution.py:62
  209.3 6.0 all-to-all-start.1
  215.3 3.3 fusion.154
  224.5 1.4 convolution_add_fusion.14
  225.9 1.4 convolution_add_fusion.12
  227.3 1.4 convolution_add_fusion.10
  228.7 1.4 convolution_add_fusion.8
  230.0 1.4 convolution_add_fusion.6
  232.8 1.4 convolution_add_fusion.2
  234.2 1.4 convolution_add_fusion
  236.4 37.7 %all-to-all-done.1 = bf16[128,72,256]{2,1,0:T(8,128)(2,1)} async-done(((bf16[128,72,256]{2,1,0:T(8,128)(2,1)}), bf16[128,72,256]{2,1,0:T(8,128)(2,1)}, u32[]{:S(2)}, u32[]{:S(2)}) %all-to-all-start.1) | async-done | bytes 4718624 | tf_op jit(solution)/shard_map/all_to_all | solution.py:61
  274.1 25.2 %gather_fusion.4 = bf16[6144,256]{1,0:T(8,128)(2,1)S(1)} fusion(bf16[9216,256]{1,0:T(8,128)(2,1)} %bitcast.6, s32[6144]{0:T(1024)} %get-tuple-element.205), kind=kCustom, calls=%fused_computation.4 | custom fusion | bytes 6316032 | tf_op jit(solution)/shard_map/gather | solution.py:64
  300.6 1.4 convolution_add_fusion.15
  302.0 1.5 convolution_add_fusion.13
  303.4 1.4 convolution_add_fusion.11
  304.9 1.4 convolution_add_fusion.9
  306.3 1.4 convolution_add_fusion.7
  307.7 1.4 convolution_add_fusion.5
  309.1 1.4 convolution_add_fusion.3
  311.9 1.7 copy.106
  313.6 1.7 copy.108
  315.3 1.8 copy.110
  317.1 1.8 copy.112
  318.8 1.7 copy.114
  320.6 1.7 copy.116
  322.3 1.7 copy.118
  324.1 1.7 copy.120
  325.8 2.1 fusion.137
  355.6 1.7 copy-done.120
  357.3 18.5 %scatter_custom_fusion.2 = f32[9216,128]{1,0:T(8,128)} fusion(s32[6144]{0:T(1024)} %copy-done.119, f32[6144,128]{1,0:T(8,128)} %bitcast.135, f32[]{:T(128)} %constant.64.clone.1), kind=kCustom, calls=%fused_computation.19 | custom fusion | bytes 4719104 | tf_op jit(solution)/shard_map/scatter | solution.py:85
  375.8 3.5 convert_element_type.154
  379.3 5.2 all-to-all-start.2
  384.6 1.7 copy.96
  386.4 1.5 convolution_add_fusion.34
  391.3 1.6 convert_reduce_fusion.6
  395.5 74.0 %all-reduce = (f32[384]{0:T(512)S(1)}, f32[384]{0:T(512)S(1)}) all-reduce(f32[384]{0:T(512)S(1)} %get-tuple-element.221, f32[384]{0:T(512)S(1)} %get-tuple-element.220), channel_id=1, replica_groups=mesh['outer'=32,'grp'=4] {'outer','grp'}, use_global_device_ids=true, to_apply=%region_17.18 | all-reduce | flops 768 | bytes 6144 | tf_op jit(solution)/shard_map/psum | solution.py:98
  470.6 72.1 %all-reduce.4.cloned.1.call-done = (f32[128,384]{1,0:T(8,128)}, f32[128,384]{1,0:T(8,128)}) async-done(((f32[128,384]{1,0:T(8,128)}, f32[128,384]{1,0:T(8,128)}), (f32[128,384]{1,0:T(8,128)}, f32[128,384]{1,0:T(8,128)})) %all-reduce.4.cloned.1.call-update) | async-done | bytes 393232 | tf_op jit(solution)/shard_map/psum | solution.py:98
  542.8 1.8 broadcast_multiply_fusion
  544.6 50.7 %scatter_custom_fusion.3 = f32[768,128]{1,0:T(8,128)} fusion(s32[9216]{0:T(1024)} %bitcast.133, bf16[9216,128]{1,0:T(8,128)(2,1)} %bitcast.28, f32[]{:T(128)} %constant.64.clone.1), kind=kCustom, calls=%fused_computation.17 | custom fusion | flops 2359296 | bytes 2753024 | tf_op jit(solution)/shard_map/scatter-add | solution.py:96
  (376 shorter events, 62.4 us)
Async XLA Ops:
  7.2 293.4 %copy-start = (bf16[128,384]{1,0:T(8,128)(2,1)S(1)}, bf16[128,384]{1,0:T(8,128)(2,1)}, u32[]{:S(2)}) copy-start(bf16[128,384]{1,0:T(8,128)(2,1)} %param.16) | copy-start | bytes 294916
  64.9 95.7 %copy-start.99 = (bf16[768,128]{1,0:T(8,128)(2,1)S(1)}, bf16[768,128]{1,0:T(8,128)(2,1)}, u32[]{:S(2)}) copy-start(bf16[768,128]{1,0:T(8,128)(2,1)} %param.15) | copy-start | bytes 589828
  65.0 95.7 %copy-start.100 = (bf16[768,128]{1,0:T(8,128)(2,1)S(1)}, bf16[768,128]{1,0:T(8,128)(2,1)}, u32[]{:S(2)}) copy-start(bf16[768,128]{1,0:T(8,128)(2,1)} %param.14) | copy-start | bytes 589828
  125.4 23.7 %copy-start.119 = (s32[6144]{0:T(1024)}, s32[6144]{0:T(1024)S(1)}, u32[]{:S(2)}) copy-start(s32[6144]{0:T(1024)S(1)} %get-tuple-element.206) | copy-start | bytes 73732
  149.1 21.1 %all-to-all-start = ((s32[128,1,72]{2,1,0:T(1,128)}), s32[128,1,72]{2,1,0:T(1,128)S(1)}, u32[]{:S(2)}, u32[]{:S(2)}) async-start(s32[128,1,72]{2,1,0:T(1,128)} %bitcast.3), calls=%async_computation | async-start | bytes 131072 | tf_op jit(solution)/shard_map/all_to_all | solution.py:59
  209.3 6.0 copy-start.4
  209.3 64.8 %all-to-all-start.1 = ((bf16[128,72,256]{2,1,0:T(8,128)(2,1)}), bf16[128,72,256]{2,1,0:T(8,128)(2,1)}, u32[]{:S(2)}, u32[]{:S(2)}) async-start(bf16[128,72,256]{2,1,0:T(8,128)(2,1)} %bitcast.129), calls=%async_computation.1 | async-start | bytes 9437184 | tf_op jit(solution)/shard_map/all_to_all | solution.py:61
  218.6 3.7 copy-start.37
  218.6 4.0 copy-start.36
  219.9 4.6 copy-start.34
  222.3 3.6 copy-start.32
  222.6 4.6 copy-start.30
  223.0 5.7 copy-start.28
  223.4 6.7 %copy-start.26 = (bf16[768,1,128]{0,2,1:T(8,128)(2,1)}, bf16[768,1,128]{0,2,1:T(8,128)(2,1)S(1)}, u32[]{:S(2)}) copy-start(bf16[768,1,128]{0,2,1:T(8,128)(2,1)S(1)} %copy.115) | copy-start | bytes 589828
  223.7 7.7 %copy-start.24 = (bf16[768,1,128]{0,2,1:T(8,128)(2,1)}, bf16[768,1,128]{0,2,1:T(8,128)(2,1)S(1)}, u32[]{:S(2)}) copy-start(bf16[768,1,128]{0,2,1:T(8,128)(2,1)S(1)} %copy.117) | copy-start | bytes 589828
  224.1 8.7 %copy-start.22 = (bf16[768,1,128]{0,2,1:T(8,128)(2,1)}, bf16[768,1,128]{0,2,1:T(8,128)(2,1)S(1)}, u32[]{:S(2)}) copy-start(bf16[768,1,128]{0,2,1:T(8,128)(2,1)S(1)} %copy.119) | copy-start | bytes 589828
  224.5 9.8 %copy-start.20 = (bf16[768,1,128]{0,2,1:T(8,128)(2,1)}, bf16[768,1,128]{0,2,1:T(8,128)(2,1)S(1)}, u32[]{:S(2)}) copy-start(bf16[768,1,128]{0,2,1:T(8,128)(2,1)S(1)} %copy.121) | copy-start | bytes 589828
  232.8 2.8 copy-start.91
  325.8 2.4 copy-start.2
  325.8 2.4 copy-start.19
  325.8 2.5 copy-start.35
  327.9 27.3 %copy-start.38 = (bf16[768,128]{0,1:T(8,128)(2,1)}, bf16[768,128]{0,1:T(8,128)(2,1)S(1)}, u32[]{:S(2)}) copy-start(bf16[768,128]{0,1:T(8,128)(2,1)S(1)} %get-tuple-element.137) | copy-start | bytes 589828
  328.6 2.6 copy-start.44
  328.6 26.6 %copy-start.40 = (bf16[768,128]{0,1:T(8,128)(2,1)}, bf16[768,128]{0,1:T(8,128)(2,1)S(1)}, u32[]{:S(2)}) copy-start(bf16[768,128]{0,1:T(8,128)(2,1)S(1)} %get-tuple-element.193) | copy-start | bytes 589828
  328.6 26.6 %copy-start.42 = (bf16[768,128]{0,1:T(8,128)(2,1)}, bf16[768,128]{0,1:T(8,128)(2,1)S(1)}, u32[]{:S(2)}) copy-start(bf16[768,128]{0,1:T(8,128)(2,1)S(1)} %get-tuple-element.194) | copy-start | bytes 589828
  331.2 23.6 %copy-start.101 = (bf16[768,128]{0,1:T(8,128)(2,1)}, bf16[768,128]{0,1:T(8,128)(2,1)S(1)}, u32[]{:S(2)}) copy-start(bf16[768,128]{0,1:T(8,128)(2,1)S(1)} %get-tuple-element.140) | copy-start | bytes 589828
  331.5 23.3 %copy-start.46 = (bf16[768,128]{0,1:T(8,128)(2,1)}, bf16[768,128]{0,1:T(8,128)(2,1)S(1)}, u32[]{:S(2)}) copy-start(bf16[768,128]{0,1:T(8,128)(2,1)S(1)} %get-tuple-element.191) | copy-start | bytes 589828
  331.5 23.3 %copy-start.47 = (bf16[768,128]{0,1:T(8,128)(2,1)}, bf16[768,128]{0,1:T(8,128)(2,1)S(1)}, u32[]{:S(2)}) copy-start(bf16[768,128]{0,1:T(8,128)(2,1)S(1)} %get-tuple-element.192) | copy-start | bytes 589828
  333.6 20.7 %copy-start.102 = (bf16[768,128]{0,1:T(8,128)(2,1)}, bf16[768,128]{0,1:T(8,128)(2,1)S(1)}, u32[]{:S(2)}) copy-start(bf16[768,128]{0,1:T(8,128)(2,1)S(1)} %get-tuple-element.143) | copy-start | bytes 589828
  334.3 20.0 %copy-start.49 = (bf16[768,128]{0,1:T(8,128)(2,1)}, bf16[768,128]{0,1:T(8,128)(2,1)S(1)}, u32[]{:S(2)}) copy-start(bf16[768,128]{0,1:T(8,128)(2,1)S(1)} %get-tuple-element.189) | copy-start | bytes 589828
  334.3 20.0 %copy-start.51 = (bf16[768,128]{0,1:T(8,128)(2,1)}, bf16[768,128]{0,1:T(8,128)(2,1)S(1)}, u32[]{:S(2)}) copy-start(bf16[768,128]{0,1:T(8,128)(2,1)S(1)} %get-tuple-element.190) | copy-start | bytes 589828
  336.4 17.5 %copy-start.104 = (bf16[768,128]{0,1:T(8,128)(2,1)}, bf16[768,128]{0,1:T(8,128)(2,1)S(1)}, u32[]{:S(2)}) copy-start(bf16[768,128]{0,1:T(8,128)(2,1)S(1)} %get-tuple-element.146) | copy-start | bytes 589828
  337.1 16.8 %copy-start.55 = (bf16[768,128]{0,1:T(8,128)(2,1)}, bf16[768,128]{0,1:T(8,128)(2,1)S(1)}, u32[]{:S(2)}) copy-start(bf16[768,128]{0,1:T(8,128)(2,1)S(1)} %get-tuple-element.187) | copy-start | bytes 589828
  337.1 16.8 %copy-start.57 = (bf16[768,128]{0,1:T(8,128)(2,1)}, bf16[768,128]{0,1:T(8,128)(2,1)S(1)}, u32[]{:S(2)}) copy-start(bf16[768,128]{0,1:T(8,128)(2,1)S(1)} %get-tuple-element.188) | copy-start | bytes 589828
  339.2 14.3 %copy-start.106 = (bf16[768,128]{0,1:T(8,128)(2,1)}, bf16[768,128]{0,1:T(8,128)(2,1)S(1)}, u32[]{:S(2)}) copy-start(bf16[768,128]{0,1:T(8,128)(2,1)S(1)} %get-tuple-element.149) | copy-start | bytes 589828
  339.9 13.6 %copy-start.63 = (bf16[768,128]{0,1:T(8,128)(2,1)}, bf16[768,128]{0,1:T(8,128)(2,1)S(1)}, u32[]{:S(2)}) copy-start(bf16[768,128]{0,1:T(8,128)(2,1)S(1)} %get-tuple-element.186) | copy-start | bytes 589828
  339.9 46.4 %copy-start.61 = (bf16[768,128]{0,1:T(8,128)(2,1)}, bf16[768,128]{0,1:T(8,128)(2,1)S(1)}, u32[]{:S(2)}) copy-start(bf16[768,128]{0,1:T(8,128)(2,1)S(1)} %get-tuple-element.185) | copy-start | bytes 589828
  342.1 11.1 %copy-start.108 = (bf16[768,128]{0,1:T(8,128)(2,1)}, bf16[768,128]{0,1:T(8,128)(2,1)S(1)}, u32[]{:S(2)}) copy-start(bf16[768,128]{0,1:T(8,128)(2,1)S(1)} %get-tuple-element.152) | copy-start | bytes 589828
  342.7 10.4 %copy-start.67 = (bf16[768,128]{0,1:T(8,128)(2,1)}, bf16[768,128]{0,1:T(8,128)(2,1)S(1)}, u32[]{:S(2)}) copy-start(bf16[768,128]{0,1:T(8,128)(2,1)S(1)} %get-tuple-element.183) | copy-start | bytes 589828
  342.8 10.4 %copy-start.70 = (bf16[768,128]{0,1:T(8,128)(2,1)}, bf16[768,128]{0,1:T(8,128)(2,1)S(1)}, u32[]{:S(2)}) copy-start(bf16[768,128]{0,1:T(8,128)(2,1)S(1)} %get-tuple-element.184) | copy-start | bytes 589828
  344.9 7.9 %copy-start.111 = (bf16[768,128]{0,1:T(8,128)(2,1)}, bf16[768,128]{0,1:T(8,128)(2,1)S(1)}, u32[]{:S(2)}) copy-start(bf16[768,128]{0,1:T(8,128)(2,1)S(1)} %get-tuple-element.155) | copy-start | bytes 589828
  345.6 7.2 %copy-start.75 = (bf16[768,128]{0,1:T(8,128)(2,1)}, bf16[768,128]{0,1:T(8,128)(2,1)S(1)}, u32[]{:S(2)}) copy-start(bf16[768,128]{0,1:T(8,128)(2,1)S(1)} %get-tuple-element.181) | copy-start | bytes 589828
  345.6 7.2 %copy-start.78 = (bf16[768,128]{0,1:T(8,128)(2,1)}, bf16[768,128]{0,1:T(8,128)(2,1)S(1)}, u32[]{:S(2)}) copy-start(bf16[768,128]{0,1:T(8,128)(2,1)S(1)} %get-tuple-element.182) | copy-start | bytes 589828
  347.7 3.0 copy-start.114
  348.4 2.3 copy-start.83
  379.3 165.2 %all-to-all-start.2 = ((bf16[128,72,128]{2,1,0:T(8,128)(2,1)}), bf16[128,72,128]{2,1,0:T(8,128)(2,1)}, u32[]{:S(2)}, u32[]{:S(2)}) async-start(bf16[128,72,128]{2,1,0:T(8,128)(2,1)} %bitcast.130), calls=%async_computation.2 | async-start | bytes 4718592 | tf_op jit(solution)/shard_map/all_to_all | solution.py:86
  384.6 158.2 %all-reduce.4.cloned.1.call-start = ((), (), s32[]{:S(2)}) async-start(), calls=%async_computation.3 | async-start | bytes 786432 | tf_op jit(solution)/shard_map/psum | solution.py:98
  390.2 2.7 copy-start.39
  (77 other events, 112.3 us)
Sparse Core Ops, SparseCore 0:
  391.4 151.3 all-reduce.3
where the time goes:
time: 610 us; the launch traced here: 602 us
  local copies, waits for them, and re-layouts  257 us (42%)
  waiting for transfers between devices  119 us (20%)
  other arithmetic  74.6 us (12%)
  blocking collectives  74 us (12%)
  matrix products  38.7 us (6%)
  starting transfers between devices  22.7 us (4%)
  between operations  15.9 us (3%)
    psum x1, blocking collectives, per_device(): lax.psum((w_in_sum, w_rec_sum, b_in_sum, b_rec_sum), ('outer', 'grp'))  74 us
    psum x1, waiting for transfers between devices, per_device(): lax.psum((w_in_sum, w_rec_sum, b_in_sum, b_rec_sum), ('outer', 'grp'))  72.1 us
    scatter-add x1, other arithmetic, per_device(): link_grad = jnp.zeros((links_dev, width), jnp.float32).at[asked_ids.resha...  50.7 us
    all_to_all x1, waiting for transfers between devices, per_device(): lax.all_to_all(link_table[clipped], ('outer', 'grp'), split_axis=0, conca...  37.7 us
    unnamed x260, local copies, waits for them, and re-layouts  37.2 us
    gather x1, local copies, waits for them, and re-layouts, per_device(): link_table[clipped]  36.9 us
    gather x1, local copies, waits for them, and re-layouts, per_device(): group_starts[sorted_owners]  36.8 us
    gather x1, local copies, waits for them, and re-layouts, per_device(): sorted_owners = owners[by_owner]  34.3 us
  transfers between devices with their start and end apart: 4, of which 3 were waited for; matrix products, arithmetic and copies ran while one was open for 5% of the time, Pallas kernels for 0%

commit v1 on v0

--- a/solution.py
+++ b/solution.py
@@ -96,7 +96,7 @@
         .add(incoming.reshape(devices * capacity, width), mode="drop")
     )
     w_in_all, w_rec_all, b_in_all, b_rec_all = lax.psum(
-        (w_in_sum, w_rec_sum, b_in_sum, b_rec_sum), ("outer", "grp")
+        lax.psum((w_in_sum, w_rec_sum, b_in_sum, b_rec_sum), "outer"), "grp"
     )
     norm_scale = 1.0 / math.sqrt(row_count * devices)
     return (

time: 610 us -> 614 us (level)
  blocking collectives: 74 us -> 80.9 us
    psum x1 -> x2, blocking collectives: 74 us -> 80.9 us  [the longest x1 69.6 us: per_device(): lax.psum((w_in_sum, w_rec_sum, b_in_sum, b_rec_sum), 'outer')]
    psum x1 -> x2, waiting for transfers between devices: 72.1 us -> 67 us  [the longest x1 41 us: per_device(): lax.psum(lax.psum((w_in_sum, w_rec_sum, b_in_sum, b_rec_sum), 'outer'), '...]
  transfers between devices with their start and end apart: 4 -> 5, of which waited for: 3 -> 4; matrix products, arithmetic and copies ran while one was open for 5% -> 5% of each run, Pallas kernels for 0% -> 0%
where the time goes in v1:
time: 614 us; the launch traced here: 604 us
  local copies, waits for them, and re-layouts  257 us (42%)
  waiting for transfers between devices  114 us (19%)
  blocking collectives  80.9 us (13%)
  other arithmetic  74.6 us (12%)
  matrix products  38.7 us (6%)
  starting transfers between devices  22.8 us (4%)
  between operations  15.9 us (3%)
    psum x1, blocking collectives, per_device(): lax.psum((w_in_sum, w_rec_sum, b_in_sum, b_rec_sum), 'outer')  69.6 us
    scatter-add x1, other arithmetic, per_device(): link_grad = jnp.zeros((links_dev, width), jnp.float32).at[asked_ids.resha...  50.7 us
    psum x1, waiting for transfers between devices, per_device(): lax.psum(lax.psum((w_in_sum, w_rec_sum, b_in_sum, b_rec_sum), 'outer'), '...  41 us
    all_to_all x1, waiting for transfers between devices, per_device(): lax.all_to_all(link_table[clipped], ('outer', 'grp'), split_axis=0, conca...  37.7 us
    unnamed x260, local copies, waits for them, and re-layouts  37.2 us
    gather x1, local copies, waits for them, and re-layouts, per_device(): link_table[clipped]  36.9 us
    gather x1, local copies, waits for them, and re-layouts, per_device(): group_starts[sorted_owners]  36.8 us
    gather x1, local copies, waits for them, and re-layouts, per_device(): sorted_owners = owners[by_owner]  34.3 us
  transfers between devices with their start and end apart: 5, of which 4 were waited for; matrix products, arithmetic and copies ran while one was open for 5% of the time, Pallas kernels for 0%

profile of v1, /device:TPU:1, one launch (start us, length us, event | category | flops | bytes accessed | tf_op | source)
XLA Modules:
  0.0 604.2 jit_solution(13778802267398426333)
XLA Ops:
  8.0 6.7 %sort.17 = (s32[6144]{0:T(1024)}, s32[6144]{0:T(1024)S(1)}) sort(s32[6144]{0:T(1024)S(1)} %get-tuple-element.212, s32[6144]{0:T(1024)S(1)} %iota.10), dimensions={0}, to_apply=%region_0.1 | sort | flops 79872 | bytes 98304 | tf_op jit(solution)/shard_map/jit(argsort)/sort | solution.py:45
  14.8 34.3 %gather_fusion.1 = s32[6144]{0:T(1024)S(1)} fusion(s32[6144]{0:T(1024)S(1)} %get-tuple-element.212, s32[6144]{0:T(1024)S(1)} %get-tuple-element.213), kind=kCustom, calls=%fused_computation.1 | custom fusion | bytes 73728 | tf_op jit(solution)/shard_map/gather | solution.py:46
  49.1 15.8 %while.24 = (s32[]{:T(128)}, u32[128]{0:T(128)S(1)}, u32[128]{0:T(128)S(1)}, s32[6144]{0:T(1024)S(1)}, s32[]{:T(128)}, /*index=5*/s32[]{:T(128)}, s32[]{}) while((s32[]{:T(128)}, u32[128]{0:T(128)S(1)}, u32[128]{0:T(128)S(1)}, s32[6144]{0:T(1024)S(1)}, s32[]{:T(128)}, /*index=5*/s32[]{:T(128)}, s32[]{}) %tuple.107), condition=%wide.region_2.3_spmd.clone, body=%wide.region_1.2_spmd.clone.sunk | while | flops 2692 | bytes 10340 | solution.py:47
  65.0 36.8 %gather_fusion.2 = s32[6144]{0:T(1024)S(1)} fusion(s32[128]{0:T(128)S(1)} %convert_element_type.136, s32[6144]{0:T(1024)S(1)} %broadcast_clamp_fusion.2), kind=kCustom, calls=%fused_computation.2 | custom fusion | bytes 73728 | tf_op jit(solution)/shard_map/gather | solution.py:53
  101.8 23.0 %scatter_custom_fusion = s32[6144]{0:T(1024)S(1)} fusion(s32[6144]{0:T(1024)S(1)} %get-tuple-element.214, s32[6144]{0:T(1024)S(1)} %add_subtract_fusion, s32[]{:T(128)} %constant.53.clone.1), kind=kCustom, calls=%fused_computation.309 | custom fusion | bytes 24580 | tf_op jit(solution)/shard_map/scatter | solution.py:55
  125.4 23.0 %scatter_custom_fusion.1 = s32[9216]{0:T(1024)S(1)} fusion(s32[6144]{0:T(1024)S(1)} %get-tuple-element.210, s32[6144]{0:T(1024)S(1)} %get-tuple-element.211, s32[]{:T(128)} %constant.52.clone.1), kind=kCustom, calls=%fused_computation.304 | custom fusion | bytes 36868 | tf_op jit(solution)/shard_map/scatter | solution.py:56
  149.1 11.5 %all-to-all-start = ((s32[128,1,72]{2,1,0:T(1,128)}), s32[128,1,72]{2,1,0:T(1,128)S(1)}, u32[]{:S(2)}, u32[]{:S(2)}) async-start(s32[128,1,72]{2,1,0:T(1,128)} %bitcast.3), calls=%async_computation | async-start | bytes 131072 | tf_op jit(solution)/shard_map/all_to_all | solution.py:59
  160.7 9.5 %all-to-all-done = s32[128,1,72]{2,1,0:T(1,128)S(1)} async-done(((s32[128,1,72]{2,1,0:T(1,128)}), s32[128,1,72]{2,1,0:T(1,128)S(1)}, u32[]{:S(2)}, u32[]{:S(2)}) %all-to-all-start) | async-done | bytes 36896 | tf_op jit(solution)/shard_map/all_to_all | solution.py:59
  170.8 1.5 fusion.155
  172.4 36.9 %gather_fusion.3 = bf16[9216,256]{1,0:T(8,128)(2,1)} fusion(bf16[768,256]{1,0:T(8,128)(2,1)S(1)} %pad_maximum_fusion.24, s32[9216]{0:T(1024)S(1)} %broadcast_clamp_fusion), kind=kCustom, calls=%fused_computation.3 | custom fusion | bytes 9474048 | tf_op jit(solution)/shard_map/gather | solution.py:62
  209.3 6.0 all-to-all-start.1
  215.3 3.3 fusion.154
  224.5 1.4 convolution_add_fusion.14
  225.9 1.4 convolution_add_fusion.12
  228.7 1.4 convolution_add_fusion.8
  232.8 1.4 convolution_add_fusion.2
  234.2 1.4 convolution_add_fusion
  236.4 37.7 %all-to-all-done.1 = bf16[128,72,256]{2,1,0:T(8,128)(2,1)} async-done(((bf16[128,72,256]{2,1,0:T(8,128)(2,1)}), bf16[128,72,256]{2,1,0:T(8,128)(2,1)}, u32[]{:S(2)}, u32[]{:S(2)}) %all-to-all-start.1) | async-done | bytes 4718624 | tf_op jit(solution)/shard_map/all_to_all | solution.py:61
  274.1 25.2 %gather_fusion.4 = bf16[6144,256]{1,0:T(8,128)(2,1)S(1)} fusion(bf16[9216,256]{1,0:T(8,128)(2,1)} %bitcast.6, s32[6144]{0:T(1024)} %get-tuple-element.209), kind=kCustom, calls=%fused_computation.4 | custom fusion | bytes 6316032 | tf_op jit(solution)/shard_map/gather | solution.py:64
  300.6 1.4 convolution_add_fusion.15
  302.0 1.5 convolution_add_fusion.13
  303.4 1.4 convolution_add_fusion.11
  304.9 1.4 convolution_add_fusion.9
  306.3 1.4 convolution_add_fusion.7
  307.7 1.4 convolution_add_fusion.5
  309.1 1.4 convolution_add_fusion.3
  311.9 1.7 copy.106
  313.6 1.7 copy.108
  315.3 1.8 copy.110
  317.1 1.8 copy.112
  318.8 1.7 copy.114
  320.6 1.7 copy.116
  322.3 1.7 copy.118
  324.1 1.7 copy.120
  325.8 2.1 fusion.137
  355.6 1.7 copy-done.120
  357.3 18.5 %scatter_custom_fusion.2 = f32[9216,128]{1,0:T(8,128)} fusion(s32[6144]{0:T(1024)} %copy-done.119, f32[6144,128]{1,0:T(8,128)} %bitcast.135, f32[]{:T(128)} %constant.64.clone.1), kind=kCustom, calls=%fused_computation.19 | custom fusion | bytes 4719104 | tf_op jit(solution)/shard_map/scatter | solution.py:85
  375.8 3.5 convert_element_type.154
  379.3 5.2 all-to-all-start.2
  384.6 1.7 copy.96
  386.4 1.5 convolution_add_fusion.34
  391.3 1.6 convert_reduce_fusion.6
  395.5 69.6 %all-reduce = (f32[384]{0:T(512)S(1)}, f32[384]{0:T(512)S(1)}) all-reduce(f32[384]{0:T(512)S(1)} %get-tuple-element.225, f32[384]{0:T(512)S(1)} %get-tuple-element.224), channel_id=1, replica_groups=mesh['outer'=32,'grp'=4] {'outer'}, use_global_device_ids=true, to_apply=%region_19.20 | all-reduce | flops 768 | bytes 6144 | tf_op jit(solution)/shard_map/psum | solution.py:99
  465.1 11.3 %all-reduce.2 = (f32[384]{0:T(512)S(1)}, f32[384]{0:T(512)S(1)}) all-reduce(f32[384]{0:T(512)S(1)} %get-tuple-element.133, f32[384]{0:T(512)S(1)} %get-tuple-element.134), channel_id=1, replica_groups=mesh['outer'=32,'grp'=4] {'grp'}, use_global_device_ids=true, to_apply=%region_20.21 | all-reduce | flops 768 | bytes 6144 | tf_op jit(solution)/shard_map/psum | solution.py:98
  476.4 26.0 %all-reduce.7.cloned.1.call-done = (f32[128,384]{1,0:T(8,128)}, f32[128,384]{1,0:T(8,128)}) async-done(((f32[128,384]{1,0:T(8,128)}, f32[128,384]{1,0:T(8,128)}), (f32[128,384]{1,0:T(8,128)}, f32[128,384]{1,0:T(8,128)})) %all-reduce.7.cloned.1.call-update) | async-done | bytes 393232 | tf_op jit(solution)/shard_map/psum | solution.py:99
  503.7 41.0 %all-reduce.9.cloned.1.call-done = (f32[128,384]{1,0:T(8,128)}, f32[128,384]{1,0:T(8,128)}) async-done(((f32[128,384]{1,0:T(8,128)}, f32[128,384]{1,0:T(8,128)}), (f32[128,384]{1,0:T(8,128)}, f32[128,384]{1,0:T(8,128)})) %all-reduce.9.cloned.1.call-update) | async-done | bytes 393232 | tf_op jit(solution)/shard_map/psum | solution.py:98
  544.6 1.8 broadcast_multiply_fusion
  546.4 50.7 %scatter_custom_fusion.3 = f32[768,128]{1,0:T(8,128)} fusion(s32[9216]{0:T(1024)} %bitcast.133, bf16[9216,128]{1,0:T(8,128)(2,1)} %bitcast.28, f32[]{:T(128)} %constant.64.clone.1), kind=kCustom, calls=%fused_computation.17 | custom fusion | flops 2359296 | bytes 2753024 | tf_op jit(solution)/shard_map/scatter-add | solution.py:96
  (380 shorter events, 65.2 us)
Async XLA Ops:
  7.2 293.4 %copy-start = (bf16[128,384]{1,0:T(8,128)(2,1)S(1)}, bf16[128,384]{1,0:T(8,128)(2,1)}, u32[]{:S(2)}) copy-start(bf16[128,384]{1,0:T(8,128)(2,1)} %param.16) | copy-start | bytes 294916
  64.9 95.7 %copy-start.99 = (bf16[768,128]{1,0:T(8,128)(2,1)S(1)}, bf16[768,128]{1,0:T(8,128)(2,1)}, u32[]{:S(2)}) copy-start(bf16[768,128]{1,0:T(8,128)(2,1)} %param.15) | copy-start | bytes 589828
  65.0 95.7 %copy-start.100 = (bf16[768,128]{1,0:T(8,128)(2,1)S(1)}, bf16[768,128]{1,0:T(8,128)(2,1)}, u32[]{:S(2)}) copy-start(bf16[768,128]{1,0:T(8,128)(2,1)} %param.14) | copy-start | bytes 589828
  125.4 23.7 %copy-start.119 = (s32[6144]{0:T(1024)}, s32[6144]{0:T(1024)S(1)}, u32[]{:S(2)}) copy-start(s32[6144]{0:T(1024)S(1)} %get-tuple-element.210) | copy-start | bytes 73732
  149.1 21.1 %all-to-all-start = ((s32[128,1,72]{2,1,0:T(1,128)}), s32[128,1,72]{2,1,0:T(1,128)S(1)}, u32[]{:S(2)}, u32[]{:S(2)}) async-start(s32[128,1,72]{2,1,0:T(1,128)} %bitcast.3), calls=%async_computation | async-start | bytes 131072 | tf_op jit(solution)/shard_map/all_to_all | solution.py:59
  209.3 6.0 copy-start.4
  209.3 64.8 %all-to-all-start.1 = ((bf16[128,72,256]{2,1,0:T(8,128)(2,1)}), bf16[128,72,256]{2,1,0:T(8,128)(2,1)}, u32[]{:S(2)}, u32[]{:S(2)}) async-start(bf16[128,72,256]{2,1,0:T(8,128)(2,1)} %bitcast.129), calls=%async_computation.1 | async-start | bytes 9437184 | tf_op jit(solution)/shard_map/all_to_all | solution.py:61
  218.6 3.7 copy-start.37
  218.6 4.0 copy-start.36
  219.9 4.6 copy-start.34
  222.3 3.6 copy-start.32
  222.6 4.6 copy-start.30
  223.0 5.7 copy-start.28
  223.4 6.7 %copy-start.26 = (bf16[768,1,128]{0,2,1:T(8,128)(2,1)}, bf16[768,1,128]{0,2,1:T(8,128)(2,1)S(1)}, u32[]{:S(2)}) copy-start(bf16[768,1,128]{0,2,1:T(8,128)(2,1)S(1)} %copy.115) | copy-start | bytes 589828
  223.7 7.7 %copy-start.24 = (bf16[768,1,128]{0,2,1:T(8,128)(2,1)}, bf16[768,1,128]{0,2,1:T(8,128)(2,1)S(1)}, u32[]{:S(2)}) copy-start(bf16[768,1,128]{0,2,1:T(8,128)(2,1)S(1)} %copy.117) | copy-start | bytes 589828
  224.1 8.7 %copy-start.22 = (bf16[768,1,128]{0,2,1:T(8,128)(2,1)}, bf16[768,1,128]{0,2,1:T(8,128)(2,1)S(1)}, u32[]{:S(2)}) copy-start(bf16[768,1,128]{0,2,1:T(8,128)(2,1)S(1)} %copy.119) | copy-start | bytes 589828
  224.5 9.8 %copy-start.20 = (bf16[768,1,128]{0,2,1:T(8,128)(2,1)}, bf16[768,1,128]{0,2,1:T(8,128)(2,1)S(1)}, u32[]{:S(2)}) copy-start(bf16[768,1,128]{0,2,1:T(8,128)(2,1)S(1)} %copy.121) | copy-start | bytes 589828
  232.8 2.8 copy-start.91
  325.8 2.4 copy-start.2
  325.8 2.4 copy-start.19
  325.8 2.5 copy-start.35
  327.9 27.3 %copy-start.38 = (bf16[768,128]{0,1:T(8,128)(2,1)}, bf16[768,128]{0,1:T(8,128)(2,1)S(1)}, u32[]{:S(2)}) copy-start(bf16[768,128]{0,1:T(8,128)(2,1)S(1)} %get-tuple-element.141) | copy-start | bytes 589828
  328.6 2.6 copy-start.44
  328.6 26.6 %copy-start.40 = (bf16[768,128]{0,1:T(8,128)(2,1)}, bf16[768,128]{0,1:T(8,128)(2,1)S(1)}, u32[]{:S(2)}) copy-start(bf16[768,128]{0,1:T(8,128)(2,1)S(1)} %get-tuple-element.197) | copy-start | bytes 589828
  328.6 26.6 %copy-start.42 = (bf16[768,128]{0,1:T(8,128)(2,1)}, bf16[768,128]{0,1:T(8,128)(2,1)S(1)}, u32[]{:S(2)}) copy-start(bf16[768,128]{0,1:T(8,128)(2,1)S(1)} %get-tuple-element.198) | copy-start | bytes 589828
  331.2 23.6 %copy-start.101 = (bf16[768,128]{0,1:T(8,128)(2,1)}, bf16[768,128]{0,1:T(8,128)(2,1)S(1)}, u32[]{:S(2)}) copy-start(bf16[768,128]{0,1:T(8,128)(2,1)S(1)} %get-tuple-element.144) | copy-start | bytes 589828
  331.5 23.3 %copy-start.46 = (bf16[768,128]{0,1:T(8,128)(2,1)}, bf16[768,128]{0,1:T(8,128)(2,1)S(1)}, u32[]{:S(2)}) copy-start(bf16[768,128]{0,1:T(8,128)(2,1)S(1)} %get-tuple-element.195) | copy-start | bytes 589828
  331.5 23.3 %copy-start.47 = (bf16[768,128]{0,1:T(8,128)(2,1)}, bf16[768,128]{0,1:T(8,128)(2,1)S(1)}, u32[]{:S(2)}) copy-start(bf16[768,128]{0,1:T(8,128)(2,1)S(1)} %get-tuple-element.196) | copy-start | bytes 589828
  333.6 20.7 %copy-start.102 = (bf16[768,128]{0,1:T(8,128)(2,1)}, bf16[768,128]{0,1:T(8,128)(2,1)S(1)}, u32[]{:S(2)}) copy-start(bf16[768,128]{0,1:T(8,128)(2,1)S(1)} %get-tuple-element.147) | copy-start | bytes 589828
  334.3 20.0 %copy-start.49 = (bf16[768,128]{0,1:T(8,128)(2,1)}, bf16[768,128]{0,1:T(8,128)(2,1)S(1)}, u32[]{:S(2)}) copy-start(bf16[768,128]{0,1:T(8,128)(2,1)S(1)} %get-tuple-element.193) | copy-start | bytes 589828
  334.3 20.0 %copy-start.51 = (bf16[768,128]{0,1:T(8,128)(2,1)}, bf16[768,128]{0,1:T(8,128)(2,1)S(1)}, u32[]{:S(2)}) copy-start(bf16[768,128]{0,1:T(8,128)(2,1)S(1)} %get-tuple-element.194) | copy-start | bytes 589828
  336.4 17.5 %copy-start.104 = (bf16[768,128]{0,1:T(8,128)(2,1)}, bf16[768,128]{0,1:T(8,128)(2,1)S(1)}, u32[]{:S(2)}) copy-start(bf16[768,128]{0,1:T(8,128)(2,1)S(1)} %get-tuple-element.150) | copy-start | bytes 589828
  337.1 16.8 %copy-start.55 = (bf16[768,128]{0,1:T(8,128)(2,1)}, bf16[768,128]{0,1:T(8,128)(2,1)S(1)}, u32[]{:S(2)}) copy-start(bf16[768,128]{0,1:T(8,128)(2,1)S(1)} %get-tuple-element.191) | copy-start | bytes 589828
  337.1 16.8 %copy-start.57 = (bf16[768,128]{0,1:T(8,128)(2,1)}, bf16[768,128]{0,1:T(8,128)(2,1)S(1)}, u32[]{:S(2)}) copy-start(bf16[768,128]{0,1:T(8,128)(2,1)S(1)} %get-tuple-element.192) | copy-start | bytes 589828
  339.2 14.3 %copy-start.106 = (bf16[768,128]{0,1:T(8,128)(2,1)}, bf16[768,128]{0,1:T(8,128)(2,1)S(1)}, u32[]{:S(2)}) copy-start(bf16[768,128]{0,1:T(8,128)(2,1)S(1)} %get-tuple-element.153) | copy-start | bytes 589828
  339.9 13.6 %copy-start.63 = (bf16[768,128]{0,1:T(8,128)(2,1)}, bf16[768,128]{0,1:T(8,128)(2,1)S(1)}, u32[]{:S(2)}) copy-start(bf16[768,128]{0,1:T(8,128)(2,1)S(1)} %get-tuple-element.190) | copy-start | bytes 589828
  339.9 46.4 %copy-start.61 = (bf16[768,128]{0,1:T(8,128)(2,1)}, bf16[768,128]{0,1:T(8,128)(2,1)S(1)}, u32[]{:S(2)}) copy-start(bf16[768,128]{0,1:T(8,128)(2,1)S(1)} %get-tuple-element.189) | copy-start | bytes 589828
  342.1 11.1 %copy-start.108 = (bf16[768,128]{0,1:T(8,128)(2,1)}, bf16[768,128]{0,1:T(8,128)(2,1)S(1)}, u32[]{:S(2)}) copy-start(bf16[768,128]{0,1:T(8,128)(2,1)S(1)} %get-tuple-element.156) | copy-start | bytes 589828
  342.7 10.4 %copy-start.67 = (bf16[768,128]{0,1:T(8,128)(2,1)}, bf16[768,128]{0,1:T(8,128)(2,1)S(1)}, u32[]{:S(2)}) copy-start(bf16[768,128]{0,1:T(8,128)(2,1)S(1)} %get-tuple-element.187) | copy-start | bytes 589828
  342.8 10.4 %copy-start.70 = (bf16[768,128]{0,1:T(8,128)(2,1)}, bf16[768,128]{0,1:T(8,128)(2,1)S(1)}, u32[]{:S(2)}) copy-start(bf16[768,128]{0,1:T(8,128)(2,1)S(1)} %get-tuple-element.188) | copy-start | bytes 589828
  344.9 7.9 %copy-start.111 = (bf16[768,128]{0,1:T(8,128)(2,1)}, bf16[768,128]{0,1:T(8,128)(2,1)S(1)}, u32[]{:S(2)}) copy-start(bf16[768,128]{0,1:T(8,128)(2,1)S(1)} %get-tuple-element.159) | copy-start | bytes 589828
  345.6 7.2 %copy-start.75 = (bf16[768,128]{0,1:T(8,128)(2,1)}, bf16[768,128]{0,1:T(8,128)(2,1)S(1)}, u32[]{:S(2)}) copy-start(bf16[768,128]{0,1:T(8,128)(2,1)S(1)} %get-tuple-element.185) | copy-start | bytes 589828
  345.6 7.2 %copy-start.78 = (bf16[768,128]{0,1:T(8,128)(2,1)}, bf16[768,128]{0,1:T(8,128)(2,1)S(1)}, u32[]{:S(2)}) copy-start(bf16[768,128]{0,1:T(8,128)(2,1)S(1)} %get-tuple-element.186) | copy-start | bytes 589828
  347.7 3.0 copy-start.114
  379.3 167.1 %all-to-all-start.2 = ((bf16[128,72,128]{2,1,0:T(8,128)(2,1)}), bf16[128,72,128]{2,1,0:T(8,128)(2,1)}, u32[]{:S(2)}, u32[]{:S(2)}) async-start(bf16[128,72,128]{2,1,0:T(8,128)(2,1)} %bitcast.130), calls=%async_computation.2 | async-start | bytes 4718592 | tf_op jit(solution)/shard_map/all_to_all | solution.py:86
  384.6 117.9 %all-reduce.7.cloned.1.call-start = ((), (), s32[]{:S(2)}) async-start(), calls=%async_computation.3 | async-start | bytes 786432 | tf_op jit(solution)/shard_map/psum | solution.py:99
  390.2 2.8 copy-start.39
  391.3 153.4 %all-reduce.9.cloned.1.call-start = ((), (), s32[]{:S(2)}) async-start(), calls=%async_computation.4 | async-start | bytes 786432 | tf_op jit(solution)/shard_map/psum | solution.py:98
  (78 other events, 115.4 us)
Sparse Core Ops, SparseCore 0:
  391.4 111.0 all-reduce.6
  504.8 39.7 all-reduce.8
